TPU v7x, 32 devices: a whole 2x2x4 slice. The times are simulated.
32 devices in a mesh: seq: 8 (over z, x), kvh: 4 (over y, core).
Axes of the slice: x: 2, y: 2, z: 4, core: 2. Of those that a mesh axis runs over, the one named last changes fastest.
Arguments:
- queries: bfloat16 [4096, 4, 4, 128], P('seq', 'kvh'), may hold values from -12 to 12
- key_states: bfloat16 [4096, 4, 128], P('seq', 'kvh'), may hold values from -10 to 10
- value_states: bfloat16 [4096, 4, 128], P('seq', 'kvh'), may hold values from -4 to 4
- grad_out: bfloat16 [4096, 4, 4, 128], P('seq', 'kvh'), may hold values from -96 to 96
- ancestors: int32 [8, 6], replicated, may hold values from -1 to 6, as said below
- query_weight: bfloat16 [8192, 4, 4, 128], P(None, 'kvh'), may hold values from -0.0625 to 0.0625
- key_weight: bfloat16 [8192, 4, 128], P(None, 'kvh'), may hold values from -0.0625 to 0.0625
- value_weight: bfloat16 [8192, 4, 128], P(None, 'kvh'), may hold values from -0.0625 to 0.0625
Outputs:
- grad_input: bfloat16 [4096, 8192], P(('seq', 'kvh'))
- grad_key: bfloat16 [4096, 4, 128], P('seq', 'kvh')
- grad_value: bfloat16 [4096, 4, 128], P('seq', 'kvh')
Inputs may be any that keep to these rules, and one draw needn't show every extreme that they name: Row b lists the strict ancestor blocks of block b, the root block 0 in slot 0 and one level deeper in each further slot, all below b; the remaining slots hold -1. Block 0 has no ancestors and is an ancestor of every other block; the blocks of every subtree are consecutive; some block has 6 ancestors.
All inputs are finite; a program needn't handle non-finite values.
Results may differ from a plain program's by a relative error of at most 0.015.
Values may be sent and summed in bfloat16 or wider, within the bound.
A program may use at most 128 MiB of HBM per device.

v0:
```python
import jax
import jax.numpy as jnp
from jax import lax
from jax.sharding import PartitionSpec as P

BLOCK = 512
DEPTH = 6


def score_block(query_block, key_block, factor):
    return (
        jnp.einsum("qgd,kd->gqk", query_block, key_block, preferred_element_type=jnp.float32)
        * factor
    )


def local(
    queries, key_states, value_states, grad_out, ancestors, query_weight, key_weight, value_weight
):
    local_rows = queries.shape[0]
    head_count = queries.shape[2]
    head_width = queries.shape[3]
    factor = head_width ** (-0.5)
    query_local = queries[:, 0]
    grad_local = grad_out[:, 0]
    pair_local = jnp.concatenate([key_states, value_states], 1)
    gathered = lax.all_gather(pair_local, "seq", axis=0, tiled=True)
    window = gathered.shape[0]
    block_count = local_rows // BLOCK
    first_block = lax.axis_index("seq") * block_count
    offsets = jnp.arange(BLOCK, dtype=jnp.int32)
    causal = (offsets[:, None] >= offsets[None, :])[None]
    carried = (jnp.zeros((window, 2, head_width), jnp.float32),)

    def deposit(carried, target, contribution):
        row_base = target * BLOCK
        current = lax.dynamic_slice_in_dim(carried[0], row_base, BLOCK, 0)
        return (lax.dynamic_update_slice_in_dim(carried[0], current + contribution, row_base, 0),)

    depth_list = []
    block_id = first_block + 0
    query_block = query_local
    grad_block = grad_local
    listed = lax.dynamic_index_in_dim(ancestors, block_id, 0, keepdims=False)
    depth_here = jnp.sum((listed >= 0).astype(jnp.int32))
    depth_list.append(depth_here)
    slot_total = DEPTH

    def fetch_slot(slot_id, listed=listed):
        target = lax.dynamic_index_in_dim(listed, slot_id, 0, keepdims=False)
        present = target >= 0
        anchor = jnp.maximum(target, 0)
        pair_block = lax.dynamic_slice_in_dim(gathered, anchor * BLOCK, BLOCK, 0)
        return (anchor, present, pair_block)

    def gather_stats(running, pair_block, visible, query_block=query_block, grad_block=grad_block):
        row_peak, total_mass, weighted = running
        scores = jnp.where(visible, score_block(query_block, pair_block[:, 0], factor), -jnp.inf)
        new_peak = jnp.maximum(row_peak, jnp.max(scores, axis=-1, keepdims=True))
        rescale = jnp.exp(row_peak - new_peak)
        exp_terms = jnp.where(visible, jnp.exp(scores - new_peak), 0.0)
        grad_probs = jnp.einsum(
            "qgd,kd->gqk", grad_block, pair_block[:, 1], preferred_element_type=jnp.float32
        )
        total_mass = total_mass * rescale + jnp.sum(exp_terms, axis=-1, keepdims=True)
        weighted = weighted * rescale + jnp.sum(exp_terms * grad_probs, axis=-1, keepdims=True)
        return (new_peak, total_mass, weighted)

    def stats_step(slot_id, running, fetch_slot=fetch_slot, gather_stats=gather_stats):
        anchor, present, pair_block = fetch_slot(slot_id)
        return gather_stats(running, pair_block, present)

    running = (
        jnp.full((head_count, BLOCK, 1), -jnp.inf, jnp.float32),
        jnp.zeros((head_count, BLOCK, 1), jnp.float32),
        jnp.zeros((head_count, BLOCK, 1), jnp.float32),
    )
    running = gather_stats(running, pair_local, causal)
    running = lax.fori_loop(0, slot_total, stats_step, running)
    log_norm = running[0] + jnp.log(running[1])
    delta_row = running[2] / running[1]

    def backward_terms(
        pair_block,
        visible,
        query_block=query_block,
        grad_block=grad_block,
        log_norm=log_norm,
        delta_row=delta_row,
    ):
        scores = score_block(query_block, pair_block[:, 0], factor)
        attn_weight = jnp.where(visible, jnp.exp(scores - log_norm), 0.0)
        grad_probs = jnp.einsum(
            "qgd,kd->gqk", grad_block, pair_block[:, 1], preferred_element_type=jnp.float32
        )
        grad_scores = (attn_weight * (grad_probs - delta_row) * factor).astype(jnp.bfloat16)
        prob_low = attn_weight.astype(jnp.bfloat16)
        query_term = jnp.einsum(
            "gqk,kd->qgd", grad_scores, pair_block[:, 0], preferred_element_type=jnp.float32
        )
        key_term = jnp.einsum(
            "gqk,qgd->kd", grad_scores, query_block, preferred_element_type=jnp.float32
        )
        value_term = jnp.einsum(
            "gqk,qgd->kd", prob_low, grad_block, preferred_element_type=jnp.float32
        )
        return (query_term, jnp.stack([key_term, value_term], 1))

    def grad_step(slot_id, loop_carry, fetch_slot=fetch_slot, backward_terms=backward_terms):
        query_total, inner_carried = loop_carry
        anchor, present, pair_block = fetch_slot(slot_id)
        query_term, pair_term = backward_terms(pair_block, present)
        return (query_total + query_term, deposit(inner_carried, anchor, pair_term))

    query_total, pair_term = backward_terms(pair_local, causal)
    carried = deposit(carried, block_id, pair_term)
    query_total, carried = lax.fori_loop(0, slot_total, grad_step, (query_total, carried))
    query_parts = query_total.astype(jnp.bfloat16)
    pair_grads = lax.psum_scatter(
        carried[0].astype(jnp.bfloat16), "seq", scatter_dimension=0, tiled=True
    )
    flat_query = query_parts.reshape(local_rows, head_count * head_width)
    query_matrix = query_weight[:, 0].reshape(query_weight.shape[0], head_count * head_width)
    key_matrix = key_weight[:, 0]
    value_matrix = value_weight[:, 0]
    contract = (((1,), (1,)), ((), ()))
    key_rows = pair_grads[:, 0]
    value_rows = pair_grads[:, 1]
    result = lax.dot_general(flat_query, query_matrix, contract, preferred_element_type=jnp.float32)
    result = result + lax.dot_general(
        key_rows, key_matrix, contract, preferred_element_type=jnp.float32
    )
    grad_input = lax.psum_scatter(
        (
            result
            + lax.dot_general(
                value_rows, value_matrix, contract, preferred_element_type=jnp.float32
            )
        ).astype(jnp.bfloat16),
        "kvh",
        scatter_dimension=0,
        tiled=True,
    )
    return (grad_input, pair_grads[:, 0:1], pair_grads[:, 1:2])


def solution(mesh):
    return jax.shard_map(
        local,
        mesh=mesh,
        in_specs=(
            P("seq", "kvh", None, None),
            P("seq", "kvh", None),
            P("seq", "kvh", None),
            P("seq", "kvh", None, None),
            P(),
            P(None, "kvh", None, None),
            P(None, "kvh", None),
            P(None, "kvh", None),
        ),
        out_specs=(P(("seq", "kvh"), None), P("seq", "kvh", None), P("seq", "kvh", None)),
        check_vma=False,
    )
```

profile of v0, /device:TPU:0, one launch (start us, length us, event | category | flops | bytes accessed | tf_op | source)
XLA Modules:
  0.0 359.7 jit_solution(15568833139301307411)
XLA Ops:
  12.0 3.6 %fusion.30 = (f32[4,512]{1,0:T(4,128)S(1)}, f32[4,512]{1,0:T(4,128)S(1)}, f32[512,512,4]{1,0,2:T(8,128)}) fusion(f32[512,512,4]{1,0,2:T(8,128)S(1)} %get-tuple-element.360, f32[4,512]{1,0:T(4,128)S(1)} %get-tuple-element.359, pred[512,512]{0,1:T(8,128)(4,1)S(1)} %iota_compare_fusion, bf16[512,1,4,128]{3,2,1,0:T(4,128)(2,1)S(1)} %copy-done.10, ...), kind=kOutput, calls=%fused_computation.47 | convolution fusion | flops 275771392 | bytes 9330688 | tf_op jit(solution)/shard_map/qgd,kd->gqk/dot_general | solution.py:62
  16.6 46.2 %all-gather.2.cloned.1.call-done = bf16[4096,2,128]{2,0,1:T(8,128)(2,1)} async-done(((bf16[512,2,128]{2,0,1:T(8,128)(2,1)}), bf16[4096,2,128]{2,0,1:T(8,128)(2,1)}) %all-gather.2.cloned.1.call-update) | async-done | bytes 2097168 | tf_op jit(solution)/shard_map/all_gather | solution.py:27
  62.8 41.1 %while.32 = (s32[]{:T(128)}, f32[4,512,1]{1,0,2:T(4,128)S(1)}, f32[4,512,1]{1,0,2:T(4,128)S(1)}, f32[4,512,1]{1,0,2:T(4,128)S(1)}, s32[6]{0:T(128)S(1)}, /*index...) while((s32[]{:T(128)}, f32[4,512,1]{1,0,2:T(4,128)S(1)}, ...), condition=%wide.region_7.8_spmd, body=%wide.region_3.7_spmd.sunk | while | flops 551557120 | bytes 16140049 | solution.py:79
  103.9 4.1 %fusion.45 = f32[512,1,128]{2,0,1:T(8,128)} fusion(f32[512,512,4]{1,0,2:T(8,128)} %copy-done.4, f32[4,512]{1,0:T(4,128)S(1)} %bitcast.256, pred[512,512]{0,1:T(8,128)(4,1)S(1)} %iota_compare_fusion, bf16[512,1,4,128]{3,2,1,0:T(4,128)(2,1)} %param.15), kind=kOutput, calls=%fused_computation.65 | convolution fusion | flops 272629760 | bytes 5251072 | tf_op jit(solution)/shard_map/gqk,qgd->kd/dot_general | solution.py:104
  108.0 3.6 fusion.33
  114.7 2.6 copy.16
  120.2 66.6 %while.33 = (s32[]{:T(128)}, f32[512,4,128]{0,2,1:T(8,128)}, f32[4096,2,128]{2,0,1:T(8,128)}, s32[6]{0:T(128)S(1)}, bf16[4096,2,128]{2,0,1:T(8,128)(2,1)}, /*ind...) while((s32[]{:T(128)}, f32[512,4,128]{0,2,1:T(8,128)}, ...), condition=%wide.region_9.10_spmd, body=%wide.region_8.9_spmd.sunk | while | flops 1354235904 | bytes 33973052 | solution.py:117
  124.6 2.4 fusion.97
  129.0 2.3 fusion.100
  135.6 2.4 fusion.97
  140.2 2.3 fusion.100
  146.8 2.4 fusion.97
  151.2 2.3 fusion.100
  157.8 2.4 fusion.97
  162.3 2.3 fusion.100
  168.9 2.4 fusion.97
  173.4 2.3 fusion.100
  180.0 2.4 fusion.97
  186.8 3.8 %convert_element_type.32 = bf16[4096,2,128]{2,0,1:T(8,128)(2,1)} convert(f32[4096,2,128]{2,0,1:T(8,128)} %get-tuple-element.303) | non-fusion elementwise | flops 1048576 | bytes 6291456 | tf_op jit(solution)/shard_map/convert_element_type | solution.py:120
  192.0 11.8 %fusion.27 = f32[512,8192]{1,0:T(8,128)} fusion(bf16[512,512]{0,1:T(8,128)(2,1)S(1)} %bitcast.254, bf16[1024,8,4,128]{3,2,1,0:T(4,128)(2,1)} %bitcast.251), kind=kOutput, calls=%fused_computation.42 | convolution fusion | flops 4294967296 | bytes 25690112 | tf_op jit(solution)/shard_map/dot_general | solution.py:129
  203.8 53.5 %reduce-scatter.3.cloned.1.call-done = bf16[512,2,128]{2,0,1:T(8,128)(2,1)} async-done(((bf16[4096,2,128]{2,0,1:T(8,128)(2,1)}), bf16[512,2,128]{2,0,1:T(8,128)(2,1)}) %reduce-scatter.3.cloned.1.call-update) | async-done | bytes 262160 | tf_op jit(solution)/shard_map/reduce_scatter | solution.py:119
  258.3 8.1 %fusion.40 = f32[512,8192]{1,0:T(8,128)} fusion(bf16[8192,1,128]{2,0,1:T(8,128)(2,1)S(1)} %copy-done, bf16[512,1,128]{2,0,1:T(8,128)(2,1)S(1)} %get-tuple-element.354), kind=kOutput, calls=%fused_computation.60 | convolution fusion | flops 1073741824 | bytes 19005440 | tf_op jit(solution)/shard_map/dot_general | solution.py:130
  266.4 15.9 %add_convert_fusion = bf16[512,8192]{1,0:T(8,128)(2,1)} fusion(f32[512,8192]{1,0:T(8,128)} %fusion.27, f32[512,8192]{1,0:T(8,128)} %fusion.40, bf16[8192,1,128]{2,0,1:T(8,128)(2,1)} %param.19, bf16[512,1,128]{2,0,1:T(8,128)(2,1)S(1)} %get-tuple-element.353), kind=kOutput, calls=%fused_computation.41 | convolution fusion | flops 1086324736 | bytes 44171264 | tf_op jit(solution)/shard_map/dot_general | solution.py:136
  282.3 70.9 %reduce-scatter.5.cloned.1.call-done = bf16[128,8192]{1,0:T(8,128)(2,1)} async-done(((bf16[512,8192]{1,0:T(8,128)(2,1)}), bf16[128,8192]{1,0:T(8,128)(2,1)}) %reduce-scatter.5.cloned.1.call-update) | async-done | bytes 2097168 | tf_op jit(solution)/shard_map/reduce_scatter | solution.py:133
  (156 shorter events, 79.5 us)
Async XLA Ops:
  7.2 251.2 %copy-start = (bf16[8192,1,128]{2,0,1:T(8,128)(2,1)S(1)}, bf16[8192,1,128]{2,0,1:T(8,128)(2,1)}, u32[]{:S(2)}) copy-start(bf16[8192,1,128]{2,0,1:T(8,128)(2,1)} %param.18) | copy-start | bytes 6291460
  7.2 4.8 %copy-start.16 = (bf16[512,1,128]{2,0,1:T(8,128)(2,1)S(1)}, bf16[512,1,128]{2,0,1:T(8,128)(2,1)}, u32[]{:S(2)}) copy-start(bf16[512,1,128]{2,0,1:T(8,128)(2,1)} %param.14) | copy-start | bytes 393220
  7.2 4.8 %copy-start.10 = (bf16[512,1,4,128]{3,2,1,0:T(4,128)(2,1)S(1)}, bf16[512,1,4,128]{3,2,1,0:T(4,128)(2,1)}, u32[]{:S(2)}) copy-start(bf16[512,1,4,128]{3,2,1,0:T(4,128)(2,1)} %param.15) | copy-start | bytes 1572868
  7.2 55.6 %all-gather.2.cloned.1.call-start = ((), (), s32[]{:S(2)}) async-start(), calls=%async_computation.2 | async-start | bytes 2359296 | tf_op jit(solution)/shard_map/all_gather | solution.py:27
  9.1 248.2 %reduce-scatter.3.cloned.1.call-start = ((), (), s32[]{:S(2)}) async-start(), calls=%async_computation.3 | async-start | bytes 2359296 | tf_op jit(solution)/shard_map/reduce_scatter | solution.py:119
  12.0 3.7 %copy-start.4 = (f32[512,512,4]{1,0,2:T(8,128)}, f32[512,512,4]{1,0,2:T(8,128)S(1)}, u32[]{:S(2)}) copy-start(f32[512,512,4]{1,0,2:T(8,128)S(1)} %get-tuple-element.360) | copy-start | bytes 12582916
  12.0 3.7 %copy-start.6 = (bf16[512,1,4,128]{3,2,1,0:T(4,128)(2,1)S(1)}, bf16[512,1,4,128]{3,2,1,0:T(4,128)(2,1)}, u32[]{:S(2)}) copy-start(bf16[512,1,4,128]{3,2,1,0:T(4,128)(2,1)} %param.12) | copy-start | bytes 1572868
  12.0 3.7 %copy-start.11 = (bf16[512,1,4,128]{3,2,1,0:T(4,128)(2,1)S(1)}, bf16[512,1,4,128]{3,2,1,0:T(4,128)(2,1)}, u32[]{:S(2)}) copy-start(bf16[512,1,4,128]{3,2,1,0:T(4,128)(2,1)} %param.15) | copy-start | bytes 1572868
  64.0 2.4 copy-start.12
  77.7 2.4 copy-start.12
  91.4 2.4 copy-start.12
  103.9 4.1 %copy-start.5 = (f32[512,512,4]{1,0,2:T(8,128)S(1)}, f32[512,512,4]{1,0,2:T(8,128)}, u32[]{:S(2)}) copy-start(f32[512,512,4]{1,0,2:T(8,128)} %copy-done.4) | copy-start | bytes 12582916
  108.0 5.0 %copy-start.7 = (bf16[512,1,128]{2,0,1:T(8,128)(2,1)S(1)}, bf16[512,1,128]{2,0,1:T(8,128)(2,1)}, u32[]{:S(2)}) copy-start(bf16[512,1,128]{2,0,1:T(8,128)(2,1)} %param.13) | copy-start | bytes 393220
  113.0 4.6 %copy-start.14 = (f32[512,1,128]{2,0,1:T(8,128)S(1)}, f32[512,1,128]{2,0,1:T(8,128)}, u32[]{:S(2)}) copy-start(f32[512,1,128]{2,0,1:T(8,128)} %fusion.45) | copy-start | bytes 786436
  114.7 5.6 %copy-start.13 = (bf16[512,4,128]{2,0,1:T(8,128)(2,1)S(1)}, bf16[512,4,128]{2,0,1:T(8,128)(2,1)}, u32[]{:S(2)}) copy-start(bf16[512,4,128]{2,0,1:T(8,128)(2,1)} %get-tuple-element.575) | copy-start | bytes 1572868
  124.5 3.1 copy-start.1
  135.6 3.1 copy-start.1
  146.7 3.1 copy-start.1
  157.8 3.1 copy-start.1
  168.9 3.1 copy-start.1
  180.0 3.1 copy-start.1
  190.6 162.5 %reduce-scatter.5.cloned.1.call-start = ((), (), s32[]{:S(2)}) async-start(), calls=%async_computation.4 | async-start | bytes 10485760 | tf_op jit(solution)/shard_map/reduce_scatter | solution.py:133
  258.3 8.1 %copy-start.9 = (bf16[512,1,128]{2,0,1:T(8,128)(2,1)}, bf16[512,1,128]{2,0,1:T(8,128)(2,1)S(1)}, u32[]{:S(2)}) copy-start(bf16[512,1,128]{2,0,1:T(8,128)(2,1)S(1)} %get-tuple-element.354) | copy-start | bytes 393220
  258.3 8.1 %copy-start.8 = (bf16[512,1,128]{2,0,1:T(8,128)(2,1)}, bf16[512,1,128]{2,0,1:T(8,128)(2,1)S(1)}, u32[]{:S(2)}) copy-start(bf16[512,1,128]{2,0,1:T(8,128)(2,1)S(1)} %get-tuple-element.353) | copy-start | bytes 393220
  (11 other events, 23.8 us)
Sparse Core Ops, SparseCore 0:
  10.8 51.9 all-gather.1
  190.8 66.4 reduce-scatter.2
  282.4 70.7 reduce-scatter.4
where the time goes:
time: 361 us; the launch traced here: 360 us
  waiting for transfers between devices  171 us (47%)
  matrix products  113 us (31%)
  other arithmetic  30.4 us (8%)
  loops' own time  16.7 us (5%)
  local copies, waits for them, and re-layouts  15.3 us (4%)
  between operations  13.9 us (4%)
    reduce_scatter x1, waiting for transfers between devices, local(): lax.psum_scatter((result + lax.dot_general(value_rows, value_matrix, cont...  70.9 us
    reduce_scatter x1, waiting for transfers between devices, local(): lax.psum_scatter(carried[0].astype(jnp.bfloat16), 'seq', scatter_dimensio...  53.5 us
    all_gather x1, waiting for transfers between devices, local(): gathered = lax.all_gather(pair_local, 'seq', axis=0, tiled=True)  46.2 us
    dot_general x13, matrix products, score_block(): jnp.einsum('qgd,kd->gqk', query_block, key_block, preferred_element_type=...  21.5 us
    dot_general x7, matrix products, gather_stats(): jnp.einsum('qgd,kd->gqk', grad_block, pair_block[:, 1], preferred_element...  16.8 us
    dot_general x1, matrix products, local(): lax.dot_general(value_rows, value_matrix, contract, preferred_element_typ...  15.9 us
    dot_general x6, matrix products, backward_terms(): jnp.einsum('qgd,kd->gqk', grad_block, pair_block[:, 1], preferred_element...  14.2 us
    dynamic_update_slice x7, other arithmetic, deposit(): lax.dynamic_update_slice_in_dim(carried[0], current + contribution, row_b...  13.8 us
  transfers between devices with their start and end apart: 3, of which 3 were waited for; matrix products, arithmetic and copies ran while one was open for 6% of the time, Pallas kernels for 0%

commit v1 on v0

--- a/solution.py
+++ b/solution.py
@@ -24,7 +24,13 @@
     query_local = queries[:, 0]
     grad_local = grad_out[:, 0]
     pair_local = jnp.concatenate([key_states, value_states], 1)
-    gathered = lax.all_gather(pair_local, "seq", axis=0, tiled=True)
+    size = lax.axis_size("seq")
+    block, blocks = (pair_local, [pair_local])
+    for _ in range(size - 1):
+        block = lax.ppermute(block, "seq", [(i, (i + 1) % size) for i in range(size)])
+        blocks.insert(0, block)
+    line = jnp.concatenate(blocks, axis=0)
+    gathered = jnp.roll(line, (lax.axis_index("seq") + 1) * pair_local.shape[0], axis=0)
     window = gathered.shape[0]
     block_count = local_rows // BLOCK
     first_block = lax.axis_index("seq") * block_count

time: 361 us -> 393 us (1.089)
  local copies, waits for them, and re-layouts: 15.3 us -> 33.6 us
  waiting for transfers between devices: 171 us -> 179 us
    ppermute x0 -> x7, waiting for transfers between devices: none -> 54.8 us  [local(): lax.ppermute(block, 'seq', [(i, (i + 1) % size) for i in range(size)])]
    all_gather x1 -> x0, waiting for transfers between devices: 46.2 us -> none  [local(): gathered = lax.all_gather(pair_local, 'seq', axis=0, tiled=True)]
    unnamed x28 -> x73, local copies, waits for them, and re-layouts: 2.67 us -> 10.6 us
  transfers between devices with their start and end apart: 3 -> 9, of which waited for: 3 -> 9; matrix products, arithmetic and copies ran while one was open for 6% -> 6% of each run, Pallas kernels for 0% -> 0%
where the time goes in v1:
time: 393 us; the launch traced here: 391 us
  waiting for transfers between devices  179 us (46%)
  matrix products  114 us (29%)
  local copies, waits for them, and re-layouts  33.6 us (9%)
  other arithmetic  30.8 us (8%)
  loops' own time  16.8 us (4%)
  between operations  14.4 us (4%)
    reduce_scatter x1, waiting for transfers between devices, local(): lax.psum_scatter((result + lax.dot_general(value_rows, value_matrix, cont...  70.8 us
    ppermute x7, waiting for transfers between devices, local(): lax.ppermute(block, 'seq', [(i, (i + 1) % size) for i in range(size)])  54.8 us
    reduce_scatter x1, waiting for transfers between devices, local(): lax.psum_scatter(carried[0].astype(jnp.bfloat16), 'seq', scatter_dimensio...  53.2 us
    dot_general x13, matrix products, score_block(): jnp.einsum('qgd,kd->gqk', query_block, key_block, preferred_element_type=...  21.6 us
    dot_general x7, matrix products, gather_stats(): jnp.einsum('qgd,kd->gqk', grad_block, pair_block[:, 1], preferred_element...  17.4 us
    dot_general x1, matrix products, local(): lax.dot_general(value_rows, value_matrix, contract, preferred_element_typ...  15.9 us
    dot_general x6, matrix products, backward_terms(): jnp.einsum('qgd,kd->gqk', grad_block, pair_block[:, 1], preferred_element...  14.3 us
    dynamic_update_slice x7, other arithmetic, deposit(): lax.dynamic_update_slice_in_dim(carried[0], current + contribution, row_b...  13.9 us
  transfers between devices with their start and end apart: 9, of which 9 were waited for; matrix products, arithmetic and copies ran while one was open for 6% of the time, Pallas kernels for 0%

profile of v1, /device:TPU:0, one launch (start us, length us, event | category | flops | bytes accessed | tf_op | source)
XLA Modules:
  0.0 391.3 jit_solution(357269059996937770)
XLA Ops:
  8.4 3.0 collective-permute-start
  11.4 9.3 %collective-permute-done = bf16[512,2,128]{2,0,1:T(8,128)(2,1)S(1)} collective-permute-done((bf16[512,2,128]{2,0,1:T(8,128)(2,1)S(1)}, bf16[512,2,128]{2,0,1:T(8,128)(2,1)S(1)}, u32[]{:S(2)}, u32[]{:S(2)}) %collective-permute-start) | collective-permute-done | bytes 262176 | tf_op jit(solution)/shard_map/ppermute | solution.py:30
  21.4 10.2 %collective-permute-done.1 = bf16[512,2,128]{2,0,1:T(8,128)(2,1)S(1)} collective-permute-done((bf16[512,2,128]{2,0,1:T(8,128)(2,1)S(1)}, bf16[512,2,128]{2,0,1:T(8,128)(2,1)S(1)}, u32[]{:S(2)}, u32[]{:S(2)}) %collective-permute-start.1) | collective-permute-done | bytes 262176 | tf_op jit(solution)/shard_map/ppermute | solution.py:30
  31.7 9.2 %collective-permute-done.2 = bf16[512,2,128]{2,0,1:T(8,128)(2,1)S(1)} collective-permute-done((bf16[512,2,128]{2,0,1:T(8,128)(2,1)S(1)}, bf16[512,2,128]{2,0,1:T(8,128)(2,1)S(1)}, u32[]{:S(2)}, u32[]{:S(2)}) %collective-permute-start.2) | collective-permute-done | bytes 262176 | tf_op jit(solution)/shard_map/ppermute | solution.py:30
  43.0 7.0 %collective-permute-done.3 = bf16[512,2,128]{2,0,1:T(8,128)(2,1)S(1)} collective-permute-done((bf16[512,2,128]{2,0,1:T(8,128)(2,1)S(1)}, bf16[512,2,128]{2,0,1:T(8,128)(2,1)S(1)}, u32[]{:S(2)}, u32[]{:S(2)}) %collective-permute-start.3) | collective-permute-done | bytes 262176 | tf_op jit(solution)/shard_map/ppermute | solution.py:30
  50.0 4.3 %fusion.30 = (f32[4,512]{1,0:T(4,128)}, f32[4,512]{1,0:T(4,128)}, f32[512,512,4]{1,0,2:T(8,128)}) fusion(f32[512,512,4]{1,0,2:T(8,128)S(1)} %get-tuple-element.360, f32[4,512]{1,0:T(4,128)S(1)} %get-tuple-element.359, pred[512,512]{0,1:T(8,128)(4,1)S(1)} %iota_compare_fusion, bf16[512,1,4,128]{3,2,1,0:T(4,128)(2,1)S(1)} %copy-done.21, ...), kind=kOutput, calls=%fused_computation.47 | convolution fusion | flops 275771392 | bytes 9330688 | tf_op jit(solution)/shard_map/qgd,kd->gqk/dot_general | solution.py:68
  54.3 4.8 %collective-permute-done.4 = bf16[512,2,128]{2,0,1:T(8,128)(2,1)} collective-permute-done((bf16[512,2,128]{2,0,1:T(8,128)(2,1)S(1)}, bf16[512,2,128]{2,0,1:T(8,128)(2,1)}, u32[]{:S(2)}, u32[]{:S(2)}) %collective-permute-start.4) | collective-permute-done | bytes 262176 | tf_op jit(solution)/shard_map/ppermute | solution.py:30
  61.8 7.1 %collective-permute-done.5 = bf16[512,2,128]{2,0,1:T(8,128)(2,1)} collective-permute-done((bf16[512,2,128]{2,0,1:T(8,128)(2,1)}, bf16[512,2,128]{2,0,1:T(8,128)(2,1)}, u32[]{:S(2)}, u32[]{:S(2)}) %collective-permute-start.5) | collective-permute-done | bytes 262176 | tf_op jit(solution)/shard_map/ppermute | solution.py:30
  70.9 7.2 %collective-permute-done.6 = bf16[512,2,128]{2,0,1:T(8,128)(2,1)S(1)} collective-permute-done((bf16[512,2,128]{2,0,1:T(8,128)(2,1)}, bf16[512,2,128]{2,0,1:T(8,128)(2,1)S(1)}, u32[]{:S(2)}, u32[]{:S(2)}) %collective-permute-start.6) | collective-permute-done | bytes 262176 | tf_op jit(solution)/shard_map/ppermute | solution.py:30
  86.9 48.4 %while.32 = (s32[]{:T(128)}, f32[4,512,1]{1,0,2:T(4,128)S(1)}, f32[4,512,1]{1,0,2:T(4,128)}, f32[4,512,1]{1,0,2:T(4,128)S(1)}, s32[6]{0:T(128)}, /*index=5*/bf16...) while((s32[]{:T(128)}, f32[4,512,1]{1,0,2:T(4,128)S(1)}, ...), condition=%wide.region_7.8_spmd, body=%wide.region_3.7_spmd.sunk | while | flops 551557120 | bytes 16205641 | solution.py:85
  136.2 4.2 %fusion.45 = f32[512,1,128]{2,0,1:T(8,128)} fusion(f32[512,512,4]{1,0,2:T(8,128)} %copy-done.5, f32[4,512]{1,0:T(4,128)S(1)} %bitcast.256, pred[512,512]{0,1:T(8,128)(4,1)S(1)} %iota_compare_fusion, bf16[512,1,4,128]{3,2,1,0:T(4,128)(2,1)} %param.15), kind=kOutput, calls=%fused_computation.65 | convolution fusion | flops 272629760 | bytes 5251072 | tf_op jit(solution)/shard_map/gqk,qgd->kd/dot_general | solution.py:110
  140.3 3.5 fusion.33
  147.1 2.6 copy.16
  152.7 66.8 %while.33 = (s32[]{:T(128)}, f32[512,4,128]{0,2,1:T(8,128)}, f32[4096,2,128]{2,0,1:T(8,128)}, s32[6]{0:T(128)S(1)}, bf16[4096,2,128]{2,0,1:T(8,128)(2,1)}, /*ind...) while((s32[]{:T(128)}, f32[512,4,128]{0,2,1:T(8,128)}, ...), condition=%wide.region_9.10_spmd, body=%wide.region_8.9_spmd.sunk | while | flops 1354235904 | bytes 33973052 | solution.py:123
  157.0 2.4 fusion.98
  179.3 2.4 fusion.98
  190.4 2.4 fusion.98
  212.7 2.4 fusion.98
  219.5 3.9 convert_element_type.32
  223.5 11.8 %fusion.27 = f32[512,8192]{1,0:T(8,128)} fusion(bf16[512,512]{0,1:T(8,128)(2,1)S(1)} %bitcast.254, bf16[1024,8,4,128]{3,2,1,0:T(4,128)(2,1)} %bitcast.251), kind=kOutput, calls=%fused_computation.42 | convolution fusion | flops 4294967296 | bytes 25690112 | tf_op jit(solution)/shard_map/dot_general | solution.py:135
  235.3 53.2 %reduce-scatter.3.cloned.1.call-done = bf16[512,2,128]{2,0,1:T(8,128)(2,1)} async-done(((bf16[4096,2,128]{2,0,1:T(8,128)(2,1)}), bf16[512,2,128]{2,0,1:T(8,128)(2,1)}) %reduce-scatter.3.cloned.1.call-update) | async-done | bytes 262160 | tf_op jit(solution)/shard_map/reduce_scatter | solution.py:125
  289.6 8.1 %fusion.40 = f32[512,8192]{1,0:T(8,128)} fusion(bf16[8192,1,128]{2,0,1:T(8,128)(2,1)S(1)} %copy-done, bf16[512,1,128]{2,0,1:T(8,128)(2,1)S(1)} %get-tuple-element.354), kind=kOutput, calls=%fused_computation.60 | convolution fusion | flops 1073741824 | bytes 19005440 | tf_op jit(solution)/shard_map/dot_general | solution.py:136
  297.7 15.9 %add_convert_fusion = bf16[512,8192]{1,0:T(8,128)(2,1)} fusion(f32[512,8192]{1,0:T(8,128)} %fusion.27, f32[512,8192]{1,0:T(8,128)} %fusion.40, bf16[8192,1,128]{2,0,1:T(8,128)(2,1)} %param.19, bf16[512,1,128]{2,0,1:T(8,128)(2,1)S(1)} %get-tuple-element.353), kind=kOutput, calls=%fused_computation.41 | convolution fusion | flops 1086324736 | bytes 44171264 | tf_op jit(solution)/shard_map/dot_general | solution.py:142
  313.6 70.8 %reduce-scatter.5.cloned.1.call-done = bf16[128,8192]{1,0:T(8,128)(2,1)} async-done(((bf16[512,8192]{1,0:T(8,128)(2,1)}), bf16[128,8192]{1,0:T(8,128)(2,1)}) %reduce-scatter.5.cloned.1.call-update) | async-done | bytes 2097168 | tf_op jit(solution)/shard_map/reduce_scatter | solution.py:139
  (238 shorter events, 114.4 us)
Async XLA Ops:
  7.2 282.4 %copy-start = (bf16[8192,1,128]{2,0,1:T(8,128)(2,1)S(1)}, bf16[8192,1,128]{2,0,1:T(8,128)(2,1)}, u32[]{:S(2)}) copy-start(bf16[8192,1,128]{2,0,1:T(8,128)(2,1)} %param.18) | copy-start | bytes 6291460
  7.2 42.8 %copy-start.9 = (bf16[512,1,128]{2,0,1:T(8,128)(2,1)S(1)}, bf16[512,1,128]{2,0,1:T(8,128)(2,1)}, u32[]{:S(2)}) copy-start(bf16[512,1,128]{2,0,1:T(8,128)(2,1)} %param.14) | copy-start | bytes 393220
  7.2 281.4 %reduce-scatter.3.cloned.1.call-start = ((), (), s32[]{:S(2)}) async-start(), calls=%async_computation.2 | async-start | bytes 2359296 | tf_op jit(solution)/shard_map/reduce_scatter | solution.py:125
  8.4 12.3 %collective-permute-start = (bf16[512,2,128]{2,0,1:T(8,128)(2,1)S(1)}, bf16[512,2,128]{2,0,1:T(8,128)(2,1)S(1)}, u32[]{:S(2)}, u32[]{:S(2)}) collective-permute-start(bf16[512,2,128]{2,0,1:T(8,128)(2,1)S(1)} %pad_maximum_fusion), channel_id=1, source_target_pairs={{0,4},{4,8},{8,12},{12,16},{16,20},{20,24},{24,28},{28,0},{1,5},{5... | collective-permute-start | bytes 786440 | tf_op jit(solution)/shard_map/ppermute | solution.py:30
  21.4 10.2 %collective-permute-start.1 = (bf16[512,2,128]{2,0,1:T(8,128)(2,1)S(1)}, bf16[512,2,128]{2,0,1:T(8,128)(2,1)S(1)}, u32[]{:S(2)}, u32[]{:S(2)}) collective-permute-start(bf16[512,2,128]{2,0,1:T(8,128)(2,1)S(1)} %collective-permute-done), channel_id=1, source_target_pairs={{0,4},{4,8},{8,12},{12,16},{16,20},{20,24},{24,28},{28,0},{1,5},{5... | collective-permute-start | bytes 786440 | tf_op jit(solution)/shard_map/ppermute | solution.py:30
  31.6 22.7 %copy-start.13 = (bf16[512,2,128]{2,0,1:T(8,128)(2,1)}, bf16[512,2,128]{2,0,1:T(8,128)(2,1)S(1)}, u32[]{:S(2)}) copy-start(bf16[512,2,128]{2,0,1:T(8,128)(2,1)S(1)} %collective-permute-done.1) | copy-start | bytes 786436
  31.6 9.3 %collective-permute-start.2 = (bf16[512,2,128]{2,0,1:T(8,128)(2,1)S(1)}, bf16[512,2,128]{2,0,1:T(8,128)(2,1)S(1)}, u32[]{:S(2)}, u32[]{:S(2)}) collective-permute-start(bf16[512,2,128]{2,0,1:T(8,128)(2,1)S(1)} %collective-permute-done.1), channel_id=1, source_target_pairs={{0,4},{4,8},{8,12},{12,16},{16,20},{20,24},{24,28},{28,0},{1,5},{5... | collective-permute-start | bytes 786440 | tf_op jit(solution)/shard_map/ppermute | solution.py:30
  31.6 18.4 %copy-start.21 = (bf16[512,1,4,128]{3,2,1,0:T(4,128)(2,1)S(1)}, bf16[512,1,4,128]{3,2,1,0:T(4,128)(2,1)}, u32[]{:S(2)}) copy-start(bf16[512,1,4,128]{3,2,1,0:T(4,128)(2,1)} %param.15) | copy-start | bytes 1572868
  40.9 9.1 %copy-start.15 = (bf16[512,2,128]{2,0,1:T(8,128)(2,1)}, bf16[512,2,128]{2,0,1:T(8,128)(2,1)S(1)}, u32[]{:S(2)}) copy-start(bf16[512,2,128]{2,0,1:T(8,128)(2,1)S(1)} %collective-permute-done.2) | copy-start | bytes 786436
  40.9 9.1 %collective-permute-start.3 = (bf16[512,2,128]{2,0,1:T(8,128)(2,1)S(1)}, bf16[512,2,128]{2,0,1:T(8,128)(2,1)S(1)}, u32[]{:S(2)}, u32[]{:S(2)}) collective-permute-start(bf16[512,2,128]{2,0,1:T(8,128)(2,1)S(1)} %collective-permute-done.2), channel_id=1, source_target_pairs={{0,4},{4,8},{8,12},{12,16},{16,20},{20,24},{24,28},{28,0},{1,5},{5... | collective-permute-start | bytes 786440 | tf_op jit(solution)/shard_map/ppermute | solution.py:30
  43.0 11.3 %copy-start.5 = (f32[512,512,4]{1,0,2:T(8,128)}, f32[512,512,4]{1,0,2:T(8,128)S(1)}, u32[]{:S(2)}) copy-start(f32[512,512,4]{1,0,2:T(8,128)S(1)} %get-tuple-element.360) | copy-start | bytes 12582916
  50.0 9.2 %collective-permute-start.4 = (bf16[512,2,128]{2,0,1:T(8,128)(2,1)S(1)}, bf16[512,2,128]{2,0,1:T(8,128)(2,1)}, u32[]{:S(2)}, u32[]{:S(2)}) collective-permute-start(bf16[512,2,128]{2,0,1:T(8,128)(2,1)S(1)} %collective-permute-done.3), channel_id=1, source_target_pairs={{0,4},{4,8},{8,12},{12,16},{16,20},{20,24},{24,28},{28,0},{1,5},{5... | collective-permute-start | bytes 786440 | tf_op jit(solution)/shard_map/ppermute | solution.py:30
  50.0 18.9 %copy-start.8 = (bf16[512,1,4,128]{3,2,1,0:T(4,128)(2,1)S(1)}, bf16[512,1,4,128]{3,2,1,0:T(4,128)(2,1)}, u32[]{:S(2)}) copy-start(bf16[512,1,4,128]{3,2,1,0:T(4,128)(2,1)} %param.12) | copy-start | bytes 1572868
  54.3 27.9 %copy-start.7 = (bf16[512,1,128]{2,0,1:T(8,128)(2,1)S(1)}, bf16[512,1,128]{2,0,1:T(8,128)(2,1)}, u32[]{:S(2)}) copy-start(bf16[512,1,128]{2,0,1:T(8,128)(2,1)} %param.13) | copy-start | bytes 393220
  59.1 9.7 %collective-permute-start.5 = (bf16[512,2,128]{2,0,1:T(8,128)(2,1)}, bf16[512,2,128]{2,0,1:T(8,128)(2,1)}, u32[]{:S(2)}, u32[]{:S(2)}) collective-permute-start(bf16[512,2,128]{2,0,1:T(8,128)(2,1)} %collective-permute-done.4), channel_id=1, source_target_pairs={{0,4},{4,8},{8,12},{12,16},{16,20},{20,24},{24,28},{28,0},{1,5},{5... | collective-permute-start | bytes 786440 | tf_op jit(solution)/shard_map/ppermute | solution.py:30
  60.4 20.8 %copy-start.16 = (bf16[512,2,128]{2,0,1:T(8,128)(2,1)S(1)}, bf16[512,2,128]{2,0,1:T(8,128)(2,1)}, u32[]{:S(2)}) copy-start(bf16[512,2,128]{2,0,1:T(8,128)(2,1)} %copy-done.15) | copy-start | bytes 786436
  60.4 20.8 %copy-start.14 = (bf16[512,2,128]{2,0,1:T(8,128)(2,1)S(1)}, bf16[512,2,128]{2,0,1:T(8,128)(2,1)}, u32[]{:S(2)}) copy-start(bf16[512,2,128]{2,0,1:T(8,128)(2,1)} %copy-done.13) | copy-start | bytes 786436
  60.4 24.8 %copy-start.18 = (bf16[512,2,128]{2,0,1:T(8,128)(2,1)S(1)}, bf16[512,2,128]{2,0,1:T(8,128)(2,1)}, u32[]{:S(2)}) copy-start(bf16[512,2,128]{2,0,1:T(8,128)(2,1)} %copy-done.17) | copy-start | bytes 786436
  68.9 9.3 %collective-permute-start.6 = (bf16[512,2,128]{2,0,1:T(8,128)(2,1)}, bf16[512,2,128]{2,0,1:T(8,128)(2,1)S(1)}, u32[]{:S(2)}, u32[]{:S(2)}) collective-permute-start(bf16[512,2,128]{2,0,1:T(8,128)(2,1)} %collective-permute-done.5), channel_id=1, source_target_pairs={{0,4},{4,8},{8,12},{12,16},{16,20},{20,24},{24,28},{28,0},{1,5},{5... | collective-permute-start | bytes 786440 | tf_op jit(solution)/shard_map/ppermute | solution.py:30
  70.9 14.4 %copy-start.12 = (bf16[512,2,128]{2,0,1:T(8,128)(2,1)S(1)}, bf16[512,2,128]{2,0,1:T(8,128)(2,1)}, u32[]{:S(2)}) copy-start(bf16[512,2,128]{2,0,1:T(8,128)(2,1)} %copy-done.11) | copy-start | bytes 786436
  70.9 14.5 %copy-start.10 = (bf16[512,1,128]{2,0,1:T(8,128)(2,1)S(1)}, bf16[512,1,128]{2,0,1:T(8,128)(2,1)}, u32[]{:S(2)}) copy-start(bf16[512,1,128]{2,0,1:T(8,128)(2,1)} %param.14) | copy-start | bytes 393220
  223.4 161.1 %reduce-scatter.5.cloned.1.call-start = ((), (), s32[]{:S(2)}) async-start(), calls=%async_computation.3 | async-start | bytes 10485760 | tf_op jit(solution)/shard_map/reduce_scatter | solution.py:139
  289.5 8.1 %copy-start.20 = (bf16[512,1,128]{2,0,1:T(8,128)(2,1)}, bf16[512,1,128]{2,0,1:T(8,128)(2,1)S(1)}, u32[]{:S(2)}) copy-start(bf16[512,1,128]{2,0,1:T(8,128)(2,1)S(1)} %get-tuple-element.354) | copy-start | bytes 393220
  289.6 8.1 %copy-start.19 = (bf16[512,1,128]{2,0,1:T(8,128)(2,1)}, bf16[512,1,128]{2,0,1:T(8,128)(2,1)S(1)}, u32[]{:S(2)}) copy-start(bf16[512,1,128]{2,0,1:T(8,128)(2,1)S(1)} %get-tuple-element.353) | copy-start | bytes 393220
  (43 other events, 115.9 us)
Sparse Core Ops, SparseCore 0:
  223.5 65.0 reduce-scatter.2
  313.7 70.6 reduce-scatter.4
